TPU v7x, 128 devices: a whole 4x4x4 slice. The times are simulated.
128 devices in a mesh: ctx: 16 (over x_lo, z, core), fsdp: 8 (over y, x_hi).
Axes of the slice: x: 4 (x_hi: 2, x_lo: 2; x = x_hi * 2 + x_lo), y: 4, z: 4, core: 2. Of those that a mesh axis runs over, the one named last changes fastest.
Arguments:
- tokens: bfloat16 [8, 2048, 1024], P('fsdp', 'ctx'), may hold values from -6 to 6
- cotangent: bfloat16 [8, 2048, 1024], P('fsdp', 'ctx'), may hold values from -6 to 6
- places: int32 [8, 2048], P('fsdp'), may hold values from 0 to 2047, as said below
- doc_split: int32 [8], P('fsdp'), may hold values from 512 to 1536
- w_query: bfloat16 [1024, 1024], P('fsdp'), may hold values from -0.1875 to 0.1875
- w_key: bfloat16 [1024, 512], P('fsdp'), may hold values from -0.1875 to 0.1875
- w_value: bfloat16 [1024, 512], P('fsdp'), may hold values from -0.1875 to 0.1875
- w_out: bfloat16 [1024, 1024], P('fsdp'), may hold values from -1 to 1
- w_gate: bfloat16 [1024, 4608], P('fsdp'), may hold values from -0.1875 to 0.1875
- w_up: bfloat16 [1024, 4608], P('fsdp'), may hold values from -0.1875 to 0.1875
- w_down: bfloat16 [4608, 1024], P('fsdp'), may hold values from -0.09375 to 0.09375
- norm_attn: bfloat16 [1024], P('fsdp'), may hold values from 0.099609375 to 1.8984375
- norm_ffn: bfloat16 [1024], P('fsdp'), may hold values from 0.099609375 to 1.8984375
- norm_query: bfloat16 [64], P('fsdp'), may hold values from 0.099609375 to 1.8984375
- norm_key: bfloat16 [64], P('fsdp'), may hold values from 0.099609375 to 1.8984375
Outputs:
- layer_out: bfloat16 [8, 2048, 1024], P('fsdp', 'ctx')
- grad_tokens: bfloat16 [8, 2048, 1024], P('fsdp', 'ctx')
- grad_w_query: float32 [1024, 1024], P('fsdp')
- grad_w_key: float32 [1024, 512], P('fsdp')
- grad_w_value: float32 [1024, 512], P('fsdp')
- grad_w_out: float32 [1024, 1024], P('fsdp')
- grad_w_gate: float32 [1024, 4608], P('fsdp')
- grad_w_up: float32 [1024, 4608], P('fsdp')
- grad_w_down: float32 [4608, 1024], P('fsdp')
- grad_norm_attn: float32 [1024], P('fsdp')
- grad_norm_ffn: float32 [1024], P('fsdp')
- grad_norm_query: float32 [64], P('fsdp')
- grad_norm_key: float32 [64], P('fsdp')
Inputs may be any that keep to these rules, and one draw needn't show every extreme that they name: In each row the places are a permutation of 0 to 2047 cut into 32 blocks of 64 places; the tokens of each device of ctx hold, in order, one block b and the block 31 - b, b drawn per row. `doc_split`: places below it form the first document of the row, the rest the second.
All inputs are finite; a program needn't handle non-finite values.
Results may differ from a plain program's by a relative error of at most 0.03.
Values may be sent and summed in bfloat16 or wider, within the bound.
No kernel may reach another device: no remote copies, remote signals or barrier semaphores. Data moves between devices by JAX's collectives and lax.ppermute only.
A program may use at most 192 MiB of HBM per device.

v0:
```python
import functools

import jax
import jax.numpy as jnp
import numpy as np
from jax import lax
from jax.experimental import pallas as pl
from jax.experimental.pallas import tpu as pltpu
from jax.sharding import Mesh
from jax.sharding import PartitionSpec as P

D = 1024
H = 16
KVH = 8
HD = 64
FF = 4608
TOK = 128
LEN = 2048
HALF = 1024
FSL = FF // 8
BLK = 64
EPS = 1e-05
THETA = 1000000.0
F32 = jnp.float32
BF16 = jnp.bfloat16
NA, NZ, NC, NY, NB = 2, 4, 2, 4, 2
CTX = ("a", "z", "c")
FS = ("y", "b")


def dot(left, right, dims=((1,), (0,))):
    return lax.dot_general(left, right, (dims, ((), ())), preferred_element_type=F32)


def shift(value, axis, size, step):
    return lax.ppermute(value, axis, [(i, (i + step) % size) for i in range(size)])


def swap(value, axis):
    return shift(value, axis, 2, 1)


def after(value, *earlier):
    return lax.optimization_barrier((value, earlier))[0]


def ring(own):
    return jnp.concatenate([own] + [shift(own, "z", NZ, step) for step in (1, 2, 3)], axis=0)


def both_cores(same):
    return jnp.concatenate([same, swap(same, "c")], axis=0)


def add_cores(mine, low, *earlier):
    return mine + after(swap(low, "c"), *earlier).astype(F32)


def add_ring(mine, *earlier):
    low = mine.astype(BF16)
    parts = [shift(low[step * TOK : (step + 1) * TOK], "z", NZ, -step) for step in (1, 2, 3)]
    if earlier:
        parts = after(parts, *earlier)
    total = mine[:TOK]
    for part in parts:
        total = total + part.astype(F32)
    return total


def heads_ring(own):
    return jnp.stack([own] + [shift(own, "z", NZ, step) for step in (1, 2, 3)])


def cross(value):
    pairs = [(m * 8 + j, j * 8 + m) for m in range(8) for j in range(8)]
    return lax.ppermute(value, ("z", "c", "y", "b"), pairs)


def fetch_shard(value):
    pairs = []
    for z, c, y, b in np.ndindex(NZ, NC, NY, NB):
        source = (((y + z) % 4 * 2 + b) * 4 + z) * 2 + c
        pairs.append((source, ((z * 2 + c) * 4 + y) * 2 + b))
    return lax.ppermute(value, ("z", "c", "y", "b"), pairs)


KC = 256


def sort_keys(kb_ref, own_ref, peer_ref, keys, values, values_one):
    for i in range(32):
        src = own_ref if i < 16 else peer_ref
        r = (i % 16) * BLK
        rows = pl.ds(pl.multiple_of(kb_ref[i] * BLK, BLK), BLK)
        block = src[r : r + BLK, :]
        keys[rows, :] = block[:, :HD]
        part = block[:, HD:]
        if values is not None:
            values[rows, :] = part
        if values_one is not None:
            values_one[rows, :] = jnp.concatenate([part, jnp.ones_like(part)], axis=1)


def key_range(p, split):
    first = jnp.where(p * BLK >= split, split // KC, 0)
    return first, (p * BLK) // KC + 1


def attention_forward_kernel(kb_ref, split_ref, q_ref, own_ref, peer_ref, out_ref, sum_ref, keys, values_one):
    sort_keys(kb_ref, own_ref, peer_ref, keys, None, values_one)
    split = split_ref[0]

    def one_block(i, _):
        p = kb_ref[i]
        rows = pl.ds(pl.multiple_of(i * BLK, BLK), BLK)
        q = jnp.concatenate([q_ref[0, rows, :], q_ref[1, rows, :]], axis=0)
        row_place = p * BLK + lax.rem(lax.broadcasted_iota(jnp.int32, (2 * BLK, KC), 0), BLK)
        start = jnp.where(row_place >= split, split, 0)
        col = lax.broadcasted_iota(jnp.int32, (2 * BLK, KC), 1)

        def one_chunk(ck, acc):
            at = pl.multiple_of(ck * KC, KC)
            s = dot(q, keys[pl.ds(at, KC), :], ((1,), (1,)))
            key_place = col + at
            seen = (key_place <= row_place) & (key_place >= start)
            e = jnp.where(seen, jnp.exp(s), 0.0).astype(BF16)
            return acc + dot(e, values_one[pl.ds(at, KC), :])

        lo, hi = key_range(p, split)
        acc = lax.fori_loop(lo, hi, one_chunk, jnp.zeros((2 * BLK, 2 * HD), F32))
        o = acc[:, :HD] / acc[:, HD:]
        out_ref[rows, :] = jnp.concatenate([o[:BLK], o[BLK:]], axis=1).astype(BF16)
        sum_ref[pl.ds(pl.multiple_of(i * 8, 8), 8), :] = acc.T[HD : HD + 8, :]
        return 0

    lax.fori_loop(0, 16, one_block, 0)


SMEM = pl.BlockSpec(memory_space=pltpu.SMEM)
VMEM = pl.BlockSpec(memory_space=pltpu.VMEM)


def attention_forward(blocks, split, queries, own, peer):
    return pl.pallas_call(
        attention_forward_kernel,
        out_shape=(
            jax.ShapeDtypeStruct((HALF, 2 * HD), BF16),
            jax.ShapeDtypeStruct((128, 128), F32),
        ),
        in_specs=[SMEM, SMEM, VMEM, VMEM, VMEM],
        out_specs=(VMEM, VMEM),
        scratch_shapes=[pltpu.VMEM((LEN, HD), BF16), pltpu.VMEM((LEN, 2 * HD), BF16)],
        compiler_params=pltpu.CompilerParams(vmem_limit_bytes=32 * 2**20),
        cost_estimate=pl.CostEstimate(flops=5 * 10**8, bytes_accessed=2 * 10**6, transcendentals=0),
    )(blocks, split, queries, own, peer)


def attention_backward_kernel(
    kb_ref, split_ref, q_ref, own_ref, peer_ref, att_ref, do_ref, sum_ref,
    dq_ref, down_ref, dpeer_ref, keys, values, keys_t, dk, dv,
):
    sort_keys(kb_ref, own_ref, peer_ref, keys, values, None)
    for i in range(LEN // KC):
        keys_t[:, i * KC : (i + 1) * KC] = keys[i * KC : (i + 1) * KC, :].T
    dk[...] = jnp.zeros_like(dk)
    dv[...] = jnp.zeros_like(dv)
    split = split_ref[0]

    def one_block(i, _):
        p = kb_ref[i]
        rows = pl.ds(pl.multiple_of(i * BLK, BLK), BLK)
        q = jnp.concatenate([q_ref[0, rows, :], q_ref[1, rows, :]], axis=0)
        pair = do_ref[rows, :]
        do = jnp.concatenate([pair[:, :HD], pair[:, HD:]], axis=0)
        prod = pair.astype(F32) * att_ref[rows, :].astype(F32)
        prod = jnp.concatenate([prod[:, :HD], prod[:, HD:]], axis=0)
        inner = jnp.sum(prod.T, axis=0, keepdims=True)
        inv = 1.0 / sum_ref[pl.ds(pl.multiple_of(i * 8, 8), 8), :][:1]
        row_place = p * BLK + lax.rem(lax.broadcasted_iota(jnp.int32, (KC, 2 * BLK), 1), BLK)
        start = jnp.where(row_place >= split, split, 0)
        col = lax.broadcasted_iota(jnp.int32, (KC, 2 * BLK), 0)

        def one_chunk(ck, dqt):
            at = pl.multiple_of(ck * KC, KC)
            here = pl.ds(at, KC)
            s = dot(keys[here, :], q, ((1,), (1,)))
            dp = dot(values[here, :], do, ((1,), (1,)))
            key_place = col + at
            seen = (key_place <= row_place) & (key_place >= start)
            prob = jnp.where(seen, jnp.exp(s), 0.0) * inv
            ds = (prob * (dp - inner)).astype(BF16)
            dv[here, :] += dot(prob.astype(BF16), do)
            dk[here, :] += dot(ds, q)
            return dqt + dot(keys_t[:, here], ds)

        lo, hi = key_range(p, split)
        dqt = lax.fori_loop(lo, hi, one_chunk, jnp.zeros((HD, 2 * BLK), F32))
        dq = (dqt.T * (HD ** -0.5)).astype(BF16)
        dq_ref[0, rows, :] = dq[:BLK]
        dq_ref[1, rows, :] = dq[BLK:]
        return 0

    lax.fori_loop(0, 16, one_block, 0)
    for i in range(32):
        rows = pl.ds(pl.multiple_of(kb_ref[i] * BLK, BLK), BLK)
        both = jnp.concatenate([dk[rows, :], dv[rows, :]], axis=1)
        r = (i % 16) * BLK
        if i < 16:
            down_ref[r : r + BLK, :] = both
        else:
            dpeer_ref[r : r + BLK, :] = both.astype(BF16)


def attention_backward(blocks, split, queries, own, peer, attended, grad, sums):
    return pl.pallas_call(
        attention_backward_kernel,
        out_shape=(
            jax.ShapeDtypeStruct((2, HALF, HD), BF16),
            jax.ShapeDtypeStruct((HALF, 2 * HD), F32),
            jax.ShapeDtypeStruct((HALF, 2 * HD), BF16),
        ),
        in_specs=[SMEM, SMEM] + [VMEM] * 6,
        out_specs=(VMEM, VMEM, VMEM),
        scratch_shapes=[
            pltpu.VMEM((LEN, HD), BF16),
            pltpu.VMEM((LEN, HD), BF16),
            pltpu.VMEM((HD, LEN), BF16),
            pltpu.VMEM((LEN, HD), F32),
            pltpu.VMEM((LEN, HD), F32),
        ],
        compiler_params=pltpu.CompilerParams(vmem_limit_bytes=32 * 2**20),
        cost_estimate=pl.CostEstimate(flops=5 * 10**8, bytes_accessed=4 * 10**6, transcendentals=0),
    )(blocks, split, queries, own, peer, attended, grad, sums)


def ffn_kernel(
    order_ref, x_ref, x_other_ref, same_ref, other_ref, weights_ref, down_ref, cot_ref, cot_other_ref, gain_ref,
    h2_ref, d_gate_ref, d_up_ref, act_ref, dh2_mine_ref, dh2_low_ref, out_mine_ref, out_low_ref,
    y1_ref, gain_grad_ref, w_out, w_gate, w_up,
):
    i = pl.program_id(0)

    @pl.when(i == 0)
    def _():
        for k in range(8):
            rows = slice(k * 128, (k + 1) * 128)
            w_out[rows, :] = weights_ref[order_ref[k], :, :D]
            w_gate[rows, :] = weights_ref[k, :, D : D + FSL]
            w_up[rows, :] = weights_ref[k, :, D + 640 : D + 640 + FSL]
        gain_grad_ref[...] = jnp.zeros_like(gain_grad_ref)

    chunks = []
    for half in range(2):
        dc, dz = i // 2, (i % 2) * 2 + half
        parts = []
        for ref, core in ((same_ref, dc), (other_ref, 1 - dc)):
            for step in range(4):
                row = (core * 4 + (dz - step + 4) % 4) * TOK
                parts.append(ref[step, pl.ds(pl.multiple_of(row, TOK), TOK), :])
        chunks.append(jnp.concatenate(parts, axis=1))
    att = jnp.concatenate(chunks, axis=0)
    x = jnp.where(i < 2, x_ref[...], x_other_ref[...]).astype(F32)
    y1 = x + dot(att, w_out[...])
    r2 = lax.rsqrt(jnp.mean(y1 * y1, axis=1, keepdims=True) + EPS)
    n2 = y1 * r2
    h2 = (n2 * gain_ref[...]).astype(BF16)
    h2_ref[...] = h2

    @pl.when(i == 0)
    def _():
        y1_ref[...] = y1[:TOK]

    gate = dot(h2, w_gate[...])
    up = dot(h2, w_up[...])
    cot = jnp.where(i < 2, cot_ref[...], cot_other_ref[...])
    da = dot(cot, down_ref[...], ((1,), (1,)))
    sg = 1.0 / (1.0 + jnp.exp(-gate))
    silu = gate * sg
    act = (silu * up).astype(BF16)
    d_up = (da * silu).astype(BF16)
    d_gate = (da * up * (sg * (1.0 + gate * (1.0 - sg)))).astype(BF16)
    act_ref[...] = act
    d_up_ref[...] = d_up
    d_gate_ref[...] = d_gate
    dh2 = dot(d_gate, w_gate[...], ((1,), (1,))) + dot(d_up, w_up[...], ((1,), (1,)))
    gain_grad_ref[...] += jnp.sum(dh2 * n2, axis=0, keepdims=True)
    out = dot(act, down_ref[...])

    @pl.when(i < 2)
    def _():
        dh2_mine_ref[...] = dh2
        out_mine_ref[...] = out

    @pl.when(i >= 2)
    def _():
        dh2_low_ref[...] = dh2.astype(BF16)
        out_low_ref[...] = out.astype(BF16)


def ffn(order, x, x_other, same, other, weights, down, cot, cot_other, gain):
    rows = 256

    tokens = pl.BlockSpec((rows, D), lambda i: (i, 0))
    hidden = pl.BlockSpec((rows, FSL), lambda i: (i, 0))
    first = pl.BlockSpec((rows, D), lambda i: (jnp.minimum(i, 1), 0))
    last = pl.BlockSpec((rows, D), lambda i: (jnp.maximum(i - 2, 0), 0))
    return pl.pallas_call(
        ffn_kernel,
        grid=(HALF // rows,),
        in_specs=[
            SMEM, first, last, whole((4, HALF, 128)), whole((4, HALF, 128)),
            whole((8, 128, 2240)), whole((FSL, D)), first, last, whole((1, D)),
        ],
        out_specs=(tokens, hidden, hidden, hidden, first, last, first, last, whole((TOK, D)), whole((1, D))),
        out_shape=(
            jax.ShapeDtypeStruct((HALF, D), BF16),
            jax.ShapeDtypeStruct((HALF, FSL), BF16),
            jax.ShapeDtypeStruct((HALF, FSL), BF16),
            jax.ShapeDtypeStruct((HALF, FSL), BF16),
            jax.ShapeDtypeStruct((512, D), F32),
            jax.ShapeDtypeStruct((512, D), BF16),
            jax.ShapeDtypeStruct((512, D), F32),
            jax.ShapeDtypeStruct((512, D), BF16),
            jax.ShapeDtypeStruct((TOK, D), F32),
            jax.ShapeDtypeStruct((1, D), F32),
        ),
        scratch_shapes=[
            pltpu.VMEM((D, D), BF16),
            pltpu.VMEM((D, FSL), BF16),
            pltpu.VMEM((D, FSL), BF16),
        ],
        compiler_params=pltpu.CompilerParams(vmem_limit_bytes=48 * 2**20),
        cost_estimate=pl.CostEstimate(flops=11 * 10**9, bytes_accessed=24 * 10**6, transcendentals=10**6),
    )(order, x, x_other, same, other, weights, down, cot, cot_other, gain)


def ffn_weights_kernel(h2_ref, cot_ref, cot_other_ref, d_gate_ref, d_up_ref, act_ref, out_ref):
    for k in range(4):
        columns = slice(k * 256, (k + 1) * 256)
        h2 = h2_ref[:, columns]
        cot = jnp.concatenate([cot_ref[:, columns], cot_other_ref[:, columns]], axis=0)
        for n, (left, right) in enumerate(((h2, d_gate_ref), (h2, d_up_ref), (cot, act_ref))):
            block = dot(left, right[...], ((0,), (0,))).astype(BF16)
            for i in range(4):
                out_ref[4 * k + i, n] = block[i * 64 : (i + 1) * 64]


def ffn_weights(h2, cot, cot_other, d_gate, d_up, act):
    return pl.pallas_call(
        ffn_weights_kernel,
        in_specs=[VMEM] * 6,
        out_specs=VMEM,
        out_shape=jax.ShapeDtypeStruct((16, 3, 64, FSL), BF16),
        compiler_params=pltpu.CompilerParams(vmem_limit_bytes=40 * 2**20),
        cost_estimate=pl.CostEstimate(flops=4 * 10**9, bytes_accessed=11 * 10**6, transcendentals=0),
    )(h2, cot, cot_other, d_gate, d_up, act)


def assemble_ffn_kernel(in_ref, gate_ref, up_ref, down_ref):
    for a in range(2):
        rows = pl.ds(a * 64, 64)
        gate_ref[rows, :] = jnp.concatenate([in_ref[a, 0, 0], in_ref[a, 1, 0]], axis=1).astype(F32)
        up_ref[rows, :] = jnp.concatenate([in_ref[a, 0, 1], in_ref[a, 1, 1]], axis=1).astype(F32)
    for i in range(2):
        block = jnp.concatenate([in_ref[0, i, 2], in_ref[1, i, 2]], axis=0).astype(F32)
        block = jnp.concatenate([block, jnp.zeros((128, 64), F32)], axis=1)
        down_ref[:, i * 128 : (i + 1) * 128] = block.T[:FSL]


def assemble_ffn(gathered):
    return pl.pallas_call(
        assemble_ffn_kernel,
        grid=(4,),
        in_specs=[pl.BlockSpec((2, 2, 3, 64, FSL), lambda i: (0, i, 0, 0, 0))],
        out_specs=(
            pl.BlockSpec((TOK, 2 * FSL), lambda i: (0, i)),
            pl.BlockSpec((TOK, 2 * FSL), lambda i: (0, i)),
            pl.BlockSpec((FSL, 256), lambda i: (0, i)),
        ),
        out_shape=(
            jax.ShapeDtypeStruct((TOK, FF), F32),
            jax.ShapeDtypeStruct((TOK, FF), F32),
            jax.ShapeDtypeStruct((FSL, D), F32),
        ),
        compiler_params=pltpu.CompilerParams(vmem_limit_bytes=32 * 2**20),
        cost_estimate=pl.CostEstimate(flops=0, bytes_accessed=11 * 10**6, transcendentals=0),
    )(gathered)


def assemble_attention_kernel(
    core_ref, same_ref, other_ref, query_ref, key_ref, value_ref, out_ref, gain_ref, stack
):
    core = core_ref[0]
    stack[core] = same_ref[...]
    stack[1 - core] = other_ref[...]
    for z in range(4):
        for c in range(2):
            m = 2 * z + c
            both = jnp.concatenate([stack[c, z, :64], stack[c, 4 + z, :64]], axis=0).astype(F32)
            query_ref[:, m * 128 : (m + 1) * 128] = both[:, :128]
            out_ref[:, m * 128 : (m + 1) * 128] = both[:, 256:].T
        for lo, ref in ((128, key_ref), (192, value_ref)):
            for a in range(2):
                ref[a * 64 : (a + 1) * 64, z * 128 : (z + 1) * 128] = jnp.concatenate(
                    [stack[c, 4 * a + z, :64, lo : lo + 64] for c in range(2)], axis=1
                ).astype(F32)
    for a in range(2):
        gain_ref[a] = sum(stack[c, 4 * a + z, 64:].astype(F32) for c in range(2) for z in range(4))


def assemble_attention(core, same, other):
    outs = pl.pallas_call(
        assemble_attention_kernel,
        out_shape=(
            jax.ShapeDtypeStruct((TOK, D), F32),
            jax.ShapeDtypeStruct((TOK, KVH * HD), F32),
            jax.ShapeDtypeStruct((TOK, KVH * HD), F32),
            jax.ShapeDtypeStruct((TOK, D), F32),
            jax.ShapeDtypeStruct((2, 16, 384), F32),
        ),
        in_specs=[SMEM, VMEM, VMEM],
        out_specs=(VMEM,) * 5,
        scratch_shapes=[pltpu.VMEM((2, 8, 80, 384), BF16)],
        compiler_params=pltpu.CompilerParams(vmem_limit_bytes=32 * 2**20),
        cost_estimate=pl.CostEstimate(flops=0, bytes_accessed=3 * 10**6, transcendentals=0),
    )(core, same, other)
    return outs[:4] + (outs[4][:, 0, :],)


def rotate(values, cosine, sine):
    half = HD // 2
    turned = jnp.concatenate([-values[:, half:], values[:, :half]], axis=1)
    return values * cosine + turned * sine


def unrotate(grads, cosine, sine):
    half = HD // 2
    scaled = grads * sine
    turned = jnp.concatenate([scaled[:, half:], -scaled[:, :half]], axis=1)
    return grads * cosine + turned


def whole(shape):
    return pl.BlockSpec(shape, lambda i: (0,) * len(shape))


def half_rows(columns):
    return (
        pl.BlockSpec((256, columns), lambda i: (jnp.minimum(i, 1), 0)),
        pl.BlockSpec((256, columns), lambda i: (jnp.maximum(i - 2, 0), 0)),
    )


def token_rows(columns):
    return pl.BlockSpec((256, columns), lambda i: (i, 0))


def project_kernel(
    x_ref, x_other_ref, weights_ref, gain_ref, gain_query_ref, gain_key_ref, cos_ref, sin_ref,
    proj_ref, query_ref, kv_ref, w_qkv,
):
    i = pl.program_id(0)

    @pl.when(i == 0)
    def _():
        for k in range(8):
            w_qkv[k * 128 : (k + 1) * 128, :] = weights_ref[k, :128, :]

    x = jnp.where(i < 2, x_ref[...], x_other_ref[...]).astype(F32)
    h1 = (x * inv_rms(x) * gain_ref[...]).astype(BF16)
    proj = dot(h1, w_qkv[...])
    proj_ref[...] = proj
    turned = []
    for h, gain in ((0, gain_query_ref), (1, gain_query_ref), (2, gain_key_ref)):
        part = proj[:, h * HD : (h + 1) * HD]
        turned.append(rotate(part * inv_rms(part) * gain[...], cos_ref[...], sin_ref[...]).astype(BF16))
    query_ref[0] = turned[0] * jnp.asarray(HD ** -0.5, BF16)
    query_ref[1] = turned[1] * jnp.asarray(HD ** -0.5, BF16)
    kv_ref[...] = jnp.concatenate([turned[2], proj[:, 3 * HD :].astype(BF16)], axis=1)


def project(x, x_other, weights, gain, gain_query, gain_key, cosine, sine):
    first, last = half_rows(D)
    return pl.pallas_call(
        project_kernel,
        grid=(4,),
        in_specs=[
            first, last, whole((8, 144, 256)), whole((1, D)), whole((1, HD)), whole((1, HD)),
            token_rows(HD), token_rows(HD),
        ],
        out_specs=(token_rows(256), pl.BlockSpec((2, 256, HD), lambda i: (0, i, 0)), token_rows(2 * HD)),
        out_shape=(
            jax.ShapeDtypeStruct((HALF, 256), F32),
            jax.ShapeDtypeStruct((2, HALF, HD), BF16),
            jax.ShapeDtypeStruct((HALF, 2 * HD), BF16),
        ),
        scratch_shapes=[pltpu.VMEM((D, 256), BF16)],
        compiler_params=pltpu.CompilerParams(vmem_limit_bytes=32 * 2**20),
        cost_estimate=pl.CostEstimate(flops=5 * 10**8, bytes_accessed=4 * 10**6, transcendentals=0),
    )(x, x_other, weights, gain, gain_query, gain_key, cosine, sine)


def project_back_kernel(
    x_ref, x_other_ref, weights_ref, gain_ref, gain_query_ref, gain_key_ref, cos_ref, sin_ref,
    proj_ref, dq_ref, dkv_ref, dkv_peer_ref,
    mine_ref, low_ref, weight_ref, gain_grad_ref, query_grad_ref, key_grad_ref, w_qkv, total,
):
    i = pl.program_id(0)

    @pl.when(i == 0)
    def _():
        for k in range(8):
            w_qkv[k * 128 : (k + 1) * 128, :] = weights_ref[k, :128, :]
        total[...] = jnp.zeros_like(total)
        for ref in (gain_grad_ref, query_grad_ref, key_grad_ref):
            ref[...] = jnp.zeros_like(ref)

    dkv = (dkv_ref[...] + dkv_peer_ref[...].astype(F32)).astype(BF16)
    grads = (dq_ref[0], dq_ref[1], dkv[:, :HD])
    outs = []
    for h, gain, grad_ref in (
        (0, gain_query_ref, query_grad_ref),
        (1, gain_query_ref, query_grad_ref),
        (2, gain_key_ref, key_grad_ref),
    ):
        part = proj_ref[:, h * HD : (h + 1) * HD]
        scale = inv_rms(part)
        normed = part * scale
        grad = unrotate(grads[h].astype(F32), cos_ref[...], sin_ref[...])
        grad_ref[...] += jnp.sum(grad * normed, axis=0, keepdims=True)
        outs.append(norm_back(grad * gain[...], normed, scale).astype(BF16))
    dqkv = jnp.concatenate(outs + [dkv[:, HD:]], axis=1)
    x = jnp.where(i < 2, x_ref[...], x_other_ref[...]).astype(F32)
    n1 = x * inv_rms(x)
    h1 = (n1 * gain_ref[...]).astype(BF16)
    dh1 = dot(dqkv, w_qkv[...], ((1,), (1,)))
    gain_grad_ref[...] += jnp.sum(dh1 * n1, axis=0, keepdims=True)
    total[...] += dot(h1, dqkv, ((0,), (0,)))

    @pl.when(i < 2)
    def _():
        mine_ref[...] = dh1

    @pl.when(i >= 2)
    def _():
        low_ref[...] = dh1.astype(BF16)

    @pl.when(i == 3)
    def _():
        weight_ref[...] = total[...].astype(BF16)


def project_back(x, x_other, weights, gain, gain_query, gain_key, cosine, sine, proj, dq, dkv, dkv_peer):
    first, last = half_rows(D)
    return pl.pallas_call(
        project_back_kernel,
        grid=(4,),
        in_specs=[
            first, last, whole((8, 144, 256)), whole((1, D)), whole((1, HD)), whole((1, HD)),
            token_rows(HD), token_rows(HD), token_rows(256),
            pl.BlockSpec((2, 256, HD), lambda i: (0, i, 0)), token_rows(2 * HD), token_rows(2 * HD),
        ],
        out_specs=(first, last, whole((D, 256)), whole((1, D)), whole((1, HD)), whole((1, HD))),
        out_shape=(
            jax.ShapeDtypeStruct((512, D), F32),
            jax.ShapeDtypeStruct((512, D), BF16),
            jax.ShapeDtypeStruct((D, 256), BF16),
            jax.ShapeDtypeStruct((1, D), F32),
            jax.ShapeDtypeStruct((1, HD), F32),
            jax.ShapeDtypeStruct((1, HD), F32),
        ),
        scratch_shapes=[pltpu.VMEM((D, 256), BF16), pltpu.VMEM((D, 256), F32)],
        compiler_params=pltpu.CompilerParams(vmem_limit_bytes=32 * 2**20),
        cost_estimate=pl.CostEstimate(flops=10**9, bytes_accessed=6 * 10**6, transcendentals=0),
    )(x, x_other, weights, gain, gain_query, gain_key, cosine, sine, proj, dq, dkv, dkv_peer)


def inv_rms(values):
    return lax.rsqrt(jnp.mean(values * values, axis=-1, keepdims=True) + EPS)


def norm_back(grads, normed, scale):
    return scale * (grads - normed * jnp.mean(grads * normed, axis=-1, keepdims=True))


def per_device(
    tokens, cotangent, places, doc_split,
    w_query, w_key, w_value, w_out, w_gate, w_up, w_down,
    norm_attn, norm_ffn, norm_query, norm_key,
):
    a, z, c = lax.axis_index("a"), lax.axis_index("z"), lax.axis_index("c")
    m = z * 2 + c
    own_tokens, own_cot = tokens[0], cotangent[0]

    gains = jnp.concatenate([norm_attn, norm_ffn, norm_query, norm_key, jnp.zeros((240,), BF16)])
    gains = jnp.concatenate([gains.reshape(2, 256), jnp.zeros((14, 256), BF16)], axis=0)
    qkv_own = jnp.concatenate(
        [
            lax.dynamic_slice_in_dim(w_query, m * 128, 128, 1),
            lax.dynamic_slice_in_dim(w_key, m * 64, 64, 1),
            lax.dynamic_slice_in_dim(w_value, m * 64, 64, 1),
        ],
        axis=1,
    )
    qkv_own = jnp.concatenate([qkv_own, gains], axis=0)
    qkv_all = lax.all_to_all(
        jnp.broadcast_to(qkv_own[None], (8, 144, 256)), FS, split_axis=0, concat_axis=0, tiled=True
    )
    w_down_m = fetch_shard(w_down)
    x_same = ring(own_tokens)
    x_other = swap(x_same, "c")
    gain_parts = qkv_all[:, 128:130].reshape(8, 512).astype(F32)
    gain_attn = gain_parts[:, :128].reshape(D)
    gain_ffn = gain_parts[:, 128:256].reshape(D)
    gain_query = gain_parts[:, 256:264].reshape(HD)
    gain_key = gain_parts[:, 264:272].reshape(HD)

    wide_own = jnp.concatenate(
        [
            w_out,
            lax.dynamic_slice_in_dim(w_gate, m * FSL, FSL, 1),
            jnp.zeros((TOK, 64), BF16),
            lax.dynamic_slice_in_dim(w_up, m * FSL, FSL, 1),
        ],
        axis=1,
    )
    wide = lax.all_gather(wide_own, FS, axis=0)

    block_of = places[0].reshape(32, BLK)[:, 0] // BLK
    wanted = []
    for half in (a, 1 - a):
        for dc in range(2):
            for dz in range(4):
                device = half * 8 + ((z - dz) % 4) * 2 + (c ^ dc)
                wanted += [device * 2, device * 2 + 1]
    wanted = jnp.stack(wanted)
    blocks = jnp.sum(
        jnp.where(wanted[:, None] == jnp.arange(32)[None, :], block_of[None, :], 0), axis=1
    ).astype(jnp.int32)
    place = (blocks[:16, None] * BLK + jnp.arange(BLK)[None, :]).reshape(HALF)
    split = doc_split[0]
    position = (place - jnp.where(place >= split, split, 0)).astype(F32)
    inv_freq = THETA ** (-2.0 * jnp.arange(HD // 2).astype(F32) / HD)
    phases = position[:, None] * inv_freq[None, :]
    phases = jnp.concatenate([phases, phases], axis=-1)
    cosine, sine = jnp.cos(phases), jnp.sin(phases)

    tables = (gain_attn[None], gain_query[None], gain_key[None], cosine, sine)
    proj, q_scaled, kv_own = project(x_same, x_other, qkv_all, *tables)
    kv_peer = swap(kv_own, "a")
    cot_same = ring(after(own_cot, kv_own))
    attended, sums = attention_forward(blocks, doc_split, q_scaled, kv_own, kv_peer)

    heads_same = heads_ring(attended)
    heads_same, cot_same, w_down_m = after((heads_same, cot_same, w_down_m))
    heads_other = swap(heads_same, "c")
    cot_other = swap(cot_same, "c")
    order = jnp.stack(
        [((z - dz) % 4) * 2 + (c ^ dc) for dc in range(2) for dz in range(4)]
    ).astype(jnp.int32)
    h2, d_gate, d_up, act, dh2_mine, dh2_low, out_mine, out_low, own_y1, grad_gain_ffn = ffn(
        order, x_same, x_other, heads_same, heads_other, wide, w_down_m, cot_same, cot_other, gain_ffn[None]
    )

    dh2_same = add_cores(dh2_mine, dh2_low)
    ffn_terms = ffn_weights(h2, cot_same, cot_other, d_gate, d_up, act)
    ffn_got = lax.all_to_all(ffn_terms, ("y", "b", "a"), split_axis=0, concat_axis=0, tiled=True)
    dh2 = add_ring(dh2_same, ffn_terms)
    own_r2 = inv_rms(own_y1)
    own_n2 = own_y1 * own_r2
    dy1 = own_cot.astype(F32) + norm_back(dh2 * gain_ffn, own_n2, own_r2)
    dz_low = dy1.astype(BF16)
    dz_same = ring(dz_low)
    dz_other = swap(dz_same, "c")
    out_same = add_cores(out_mine, after(out_low, dz_same))

    w_out_m = lax.dynamic_index_in_dim(wide, m, 0, keepdims=False)[:, :D]
    d_att = jnp.concatenate(
        [dot(part, w_out_m, ((1,), (1,))).astype(BF16) for part in (dz_same, dz_other)], axis=0
    )
    dq_rot, dkv_own, dkv_peer = attention_backward(
        blocks, doc_split, q_scaled, kv_own, kv_peer, attended, d_att, sums
    )
    layer_out = (own_y1 + add_ring(out_same)).astype(BF16)
    dkv_peer = swap(dkv_peer, "a")
    ffn_piece = jnp.sum(after(ffn_got, dq_rot).astype(F32), axis=0).astype(BF16)
    ffn_piece = jnp.concatenate([ffn_piece[:2], cross(ffn_piece[2])[None]], axis=0)
    dkv_peer, ffn_piece = after((dkv_peer, ffn_piece))
    ffn_all = lax.all_gather(ffn_piece, CTX, axis=0).reshape(2, 8, 3, 64, FSL)
    out_terms = dot(dz_same, attended[:512], ((0,), (0,))) + dot(dz_other, attended[512:], ((0,), (0,)))
    dh1_mine, dh1_low, qkv_terms, grad_gain_attn, grad_gain_query, grad_gain_key = project_back(
        x_same, x_other, qkv_all, *tables, proj, dq_rot, dkv_own, dkv_peer
    )

    attn_terms = jnp.concatenate([qkv_terms, out_terms.astype(BF16)], axis=1)
    gain_terms = jnp.concatenate(
        [
            grad_gain_attn.reshape(8, 128),
            grad_gain_ffn.reshape(8, 128),
            grad_gain_query.reshape(8, 8),
            grad_gain_key.reshape(8, 8),
        ],
        axis=1,
    ).reshape(8, 2, 1, 136)
    gain_terms = jnp.pad(gain_terms, ((0, 0), (0, 0), (0, 15), (0, 384 - 136)))
    terms = jnp.concatenate([attn_terms.reshape(8, 2, 64, 384), gain_terms.astype(BF16)], axis=2)
    terms = terms.reshape(16, 80, 384)
    dh1_same = add_cores(dh1_mine, dh1_low, terms)
    dh1 = add_ring(dh1_same)
    own_x = own_tokens.astype(F32)
    own_r1 = inv_rms(own_x)
    grad_tokens = (dy1 + norm_back(dh1 * gain_attn, own_x * own_r1, own_r1)).astype(BF16)
    got = lax.all_to_all(terms, ("y", "b", "a"), split_axis=0, concat_axis=0, tiled=True)
    piece = jnp.sum(after(got, dh1_same).astype(F32), axis=0).astype(BF16)
    piece = jnp.concatenate([piece[:, :256], cross(piece[:, 256:])], axis=1)
    piece, grad_tokens = after((piece, grad_tokens))
    ffn_grads = assemble_ffn(ffn_all)
    piece, ffn_grads, layer_out = after((piece, ffn_grads, layer_out))
    grad_gate, grad_up, grad_down = ffn_grads
    same = lax.all_to_all(
        jnp.broadcast_to(piece[None], (8, 80, 384)), ("a", "z"), split_axis=0, concat_axis=0, tiled=True
    )
    first_core = jnp.full((1,), c, jnp.int32)
    grad_query, grad_key, grad_value, grad_out, gain_sum = assemble_attention(
        first_core, same, swap(same, "c")
    )
    gain_sum = gain_sum[:, :136].reshape(272)
    return (
        layer_out[None],
        grad_tokens[None],
        grad_query,
        grad_key,
        grad_value,
        grad_out,
        grad_gate,
        grad_up,
        grad_down,
        gain_sum[:128],
        gain_sum[128:256],
        gain_sum[256:264],
        gain_sum[264:],
    )


def solution(mesh):
    fine = Mesh(mesh.devices.reshape(NA, NZ, NC, NY, NB), CTX + FS)
    rows = P(FS, CTX, None)
    shard = P(FS, None)
    in_specs = (rows, rows, shard, P(FS)) + (shard,) * 7 + (P(FS),) * 4
    out_specs = (rows, rows) + (shard,) * 7 + (P(FS),) * 4
    return jax.shard_map(
        per_device, mesh=fine, in_specs=in_specs, out_specs=out_specs, check_vma=False
    )
```

profile of v0, /device:TPU:1, one launch (start us, length us, event | category | flops | bytes accessed | tf_op | source)
XLA Modules:
  0.0 340.6 jit_solution(4252919686208634259)
XLA Ops:
  11.5 4.6 %collective-permute-start.2 = (bf16[128,1024]{1,0:T(8,128)(2,1)S(1)}, bf16[128,1024]{1,0:T(8,128)(2,1)S(1)}, u32[]{:S(2)}, u32[]{:S(2)}) collective-permute-start(bf16[128,1024]{1,0:T(8,128)(2,1)S(1)} %bitcast.97), channel_id=1, source_target_pairs={{0,48},{16,0},{32,16},{48,32},{1,49},{17,1},{33,17},{49,33},{2,50}... | collective-permute-start | bytes 786440 | tf_op jit(solution)/shard_map/ppermute | solution.py:36
  20.5 6.7 %all-to-all-start = ((bf16[8,144,256]{2,1,0:T(8,128)(2,1)}), bf16[8,144,256]{2,1,0:T(8,128)(2,1)S(1)}, u32[]{:S(2)}, u32[]{:S(2)}) async-start(bf16[8,144,256]{2,1,0:T(8,128)(2,1)} %broadcast_in_dim.64), calls=%async_computation | async-start | bytes 1179648 | tf_op jit(solution)/shard_map/all_to_all | solution.py:606
  27.1 6.8 %collective-permute-start.11 = (bf16[576,1024]{1,0:T(8,128)(2,1)}, bf16[576,1024]{1,0:T(8,128)(2,1)}, u32[]{:S(2)}, u32[]{:S(2)}) collective-permute-start(bf16[576,1024]{1,0:T(8,128)(2,1)} %param.25), channel_id=1, source_target_pairs={{0,0},{8,1},{16,2},{24,3},{32,4},{40,5},{48,6},{56,7},{1,8},{9,9},... | collective-permute-start | bytes 3538952 | tf_op jit(solution)/shard_map/ppermute | solution.py:84
  36.7 5.4 %collective-permute-start.3 = (bf16[512,1024]{1,0:T(8,128)(2,1)S(1)}, bf16[512,1024]{1,0:T(8,128)(2,1)}, u32[]{:S(2)}, u32[]{:S(2)}) collective-permute-start(bf16[512,1024]{1,0:T(8,128)(2,1)S(1)} %pad_maximum_fusion.x_ref), channel_id=1, source_target_pairs={{0,8},{8,0},{1,9},{9,1},{2,10},{10,2},{3,11},{11,3},{4,12},{12,4},... | collective-permute-start | bytes 3145736 | tf_op jit(solution)/shard_map/ppermute | solution.py:36
  45.3 7.4 %shard_map.246 = (f32[1024,256]{1,0:T(8,128)S(1)}, bf16[2,1024,64]{2,1,0:T(8,128)(2,1)S(1)}, bf16[1024,128]{1,0:T(8,128)(2,1)S(1)}) custom-call(bf16[512,1024]{1,0:T(8,128)(2,1)S(1)} %pad_maximum_fusion.x_ref, bf16[512,1024]{1,0:T(8,128)(2,1)} %collective-permute-done.3.x_other_ref, bf16[8,144,256]{2,1,0:T(8,128)(2,1)S(1)} %all-to-all-done.weights_ref, ...), custom_call_target="tpu_custom_call" | custom-call | flops 500000000 | bytes 4000000 | tf_op jit(solution)/shard_map/pallas_call | solution.py:484
  56.8 4.7 %collective-permute-done.4.peer_ref = bf16[1024,128]{1,0:T(8,128)(2,1)S(1)} collective-permute-done((bf16[1024,128]{1,0:T(8,128)(2,1)S(1)}, bf16[1024,128]{1,0:T(8,128)(2,1)S(1)}, u32[]{:S(2)}, u32[]{:S(2)}) %collective-permute-start.4) | collective-permute-done | bytes 262176 | tf_op jit(solution)/shard_map/ppermute | solution.py:36
  61.4 16.4 %shard_map.247 = (bf16[1024,128]{1,0:T(8,128)(2,1)S(1)}, f32[128,128]{1,0:T(8,128)S(1)}) custom-call(s32[32]{0:T(128)S(1)} %select_reduce_fusion.kb_ref, s32[1]{0:T(128)} %copy.48.split_ref, bf16[2,1024,64]{2,1,0:T(8,128)(2,1)S(1)} %get-tuple-element.66.q_ref, bf16[1024,128]{1,0:T(8,128)(2,1)S(1)} %get-tuple-element.67.own_ref, ...), custom_call_target="tpu_custom_call" | custom-call | flops 500000000 | bytes 2000000 | tf_op jit(solution)/shard_map/pallas_call | solution.py:144
  80.8 4.1 %collective-permute-done.7 = bf16[1024,128]{1,0:T(8,128)(2,1)S(1)} collective-permute-done((bf16[1024,128]{1,0:T(8,128)(2,1)S(1)}, bf16[1024,128]{1,0:T(8,128)(2,1)S(1)}, u32[]{:S(2)}, u32[]{:S(2)}) %collective-permute-start.7) | collective-permute-done | bytes 262176 | tf_op jit(solution)/shard_map/ppermute | solution.py:36
  85.9 8.2 %collective-permute-done.5 = bf16[1024,128]{1,0:T(8,128)(2,1)S(1)} collective-permute-done((bf16[1024,128]{1,0:T(8,128)(2,1)S(1)}, bf16[1024,128]{1,0:T(8,128)(2,1)S(1)}, u32[]{:S(2)}, u32[]{:S(2)}) %collective-permute-start.5) | collective-permute-done | bytes 262176 | tf_op jit(solution)/shard_map/ppermute | solution.py:36
  99.8 8.7 %all-gather.5.cloned.1.call-done = bf16[1024,2240]{1,0:T(8,128)(2,1)} async-done(((bf16[128,2240]{1,0:T(8,128)(2,1)}), bf16[1024,2240]{1,0:T(8,128)(2,1)}) %all-gather.5.cloned.1.call-update) | async-done | bytes 4587536 | tf_op jit(solution)/shard_map/all_gather | solution.py:627
  108.5 23.1 %shard_map.248 = (bf16[1024,1024]{1,0:T(8,128)(2,1)}, bf16[1024,576]{1,0:T(8,128)(2,1)}, bf16[1024,576]{1,0:T(8,128)(2,1)}, bf16[1024,576]{1,0:T(8,128)(2,1)}, f...) custom-call(s32[8]{0:T(128)S(1)} %stack.182.order_ref, ...), custom_call_target="tpu_custom_call" | custom-call | flops 11000000512 | bytes 24000000 | tf_op jit(solution)/shard_map/pallas_call | solution.py:307
  139.1 6.6 %shard_map.249 = bf16[16,3,64,576]{3,2,1,0:T(8,128)(2,1)S(1)} custom-call(bf16[1024,1024]{1,0:T(8,128)(2,1)S(1)} %copy-done.23, bf16[512,1024]{1,0:T(8,128)(2,1)} %pad_maximum_fusion.2.cot_ref, bf16[512,1024]{1,0:T(8,128)(2,1)} %collective-permute-done.13.cot_other_ref, bf16[1024,576]{1,0:T(8,128)(2,1)S(1)} %copy-done.24, bf16[1024,576]{1,0:T(8,128)(2,1)S(1)} %copy-done.25, ...), custom_call_target="tpu_custom_call" | custom-call | flops 4000000000 | bytes 11000000 | tf_op jit(solution)/shard_map/pallas_call | solution.py:349
  147.8 5.8 %all-to-all-start.1 = ((bf16[16,3,64,576]{3,2,1,0:T(8,128)(2,1)}), bf16[16,3,64,576]{3,2,1,0:T(8,128)(2,1)}, u32[]{:S(2)}, u32[]{:S(2)}) async-start(bf16[16,3,64,576]{3,2,1,0:T(8,128)(2,1)} %copy-done.3), calls=%async_computation.1 | async-start | bytes 7864320 | tf_op jit(solution)/shard_map/all_to_all | solution.py:667
  159.3 4.3 %collective-permute-done.15 = bf16[128,1024]{1,0:T(8,128)(2,1)S(1)} collective-permute-done((bf16[128,1024]{1,0:T(8,128)(2,1)S(1)}, bf16[128,1024]{1,0:T(8,128)(2,1)S(1)}, u32[]{:S(2)}, u32[]{:S(2)}) %collective-permute-start.15) | collective-permute-done | bytes 262176 | tf_op jit(solution)/shard_map/ppermute | solution.py:36
  166.6 6.2 %collective-permute-done.17 = bf16[128,1024]{1,0:T(8,128)(2,1)S(1)} collective-permute-done((bf16[128,1024]{1,0:T(8,128)(2,1)S(1)}, bf16[128,1024]{1,0:T(8,128)(2,1)S(1)}, u32[]{:S(2)}, u32[]{:S(2)}) %collective-permute-start.17) | collective-permute-done | bytes 262176 | tf_op jit(solution)/shard_map/ppermute | solution.py:36
  176.1 5.6 %collective-permute-done.20 = bf16[128,1024]{1,0:T(8,128)(2,1)S(1)} collective-permute-done((bf16[128,1024]{1,0:T(8,128)(2,1)S(1)}, bf16[128,1024]{1,0:T(8,128)(2,1)S(1)}, u32[]{:S(2)}, u32[]{:S(2)}) %collective-permute-start.20) | collective-permute-done | bytes 262176 | tf_op jit(solution)/shard_map/ppermute | solution.py:36
  182.6 7.0 %collective-permute-done.18 = bf16[128,1024]{1,0:T(8,128)(2,1)S(1)} collective-permute-done((bf16[128,1024]{1,0:T(8,128)(2,1)S(1)}, bf16[128,1024]{1,0:T(8,128)(2,1)S(1)}, u32[]{:S(2)}, u32[]{:S(2)}) %collective-permute-start.18) | collective-permute-done | bytes 262176 | tf_op jit(solution)/shard_map/ppermute | solution.py:36
  195.6 20.1 %shard_map.250 = (bf16[2,1024,64]{2,1,0:T(8,128)(2,1)S(1)}, f32[1024,128]{1,0:T(8,128)S(1)}, bf16[1024,128]{1,0:T(8,128)(2,1)}) custom-call(s32[32]{0:T(128)S(1)} %select_reduce_fusion.kb_ref, s32[1]{0:T(128)} %copy.48.split_ref, bf16[2,1024,64]{2,1,0:T(8,128)(2,1)S(1)} %copy-done.16, bf16[1024,128]{1,0:T(8,128)(2,1)S(1)} %copy-done.18, ...), custom_call_target="tpu_custom_call" | custom-call | flops 500000000 | bytes 4000000 | tf_op jit(solution)/shard_map/pallas_call | solution.py:215
  224.4 6.2 %collective-permute-start.23 = (bf16[64,576]{1,0:T(8,128)(2,1)S(1)}, bf16[64,576]{1,0:T(8,128)(2,1)S(1)}, u32[]{:S(2)}, u32[]{:S(2)}) collective-permute-start(bf16[64,576]{1,0:T(8,128)(2,1)S(1)} %slice_bitcast_fusion), channel_id=1, source_target_pairs={{0,0},{1,8},{2,16},{3,24},{4,32},{5,40},{6,48},{7,56},{8,1},{9,9},... | collective-permute-start | bytes 221192 | tf_op jit(solution)/shard_map/ppermute | solution.py:76
  240.8 10.9 %shard_map.251 = (f32[512,1024]{1,0:T(8,128)S(1)}, bf16[512,1024]{1,0:T(8,128)(2,1)}, bf16[1024,256]{1,0:T(8,128)(2,1)S(1)}, f32[1,1024]{1,0:T(1,128)S(1)}, f32[1,64]{1,0:T(1,128)S(1)}, /*index=5*/f32[1,64]{1,0:T(1,128)S(1)}) custom-call(bf16[512,1024]{1,0:T(8,128)(2,1)S(1)} %pad_maximum_fusion.x_ref, bf16[512,1024]{1,0:T(8,128)(2,1)} %collective-permute-done.3.x_other_ref, ...), custom_call_target="tpu_custom_call" | custom-call | flops 1000000000 | bytes 6000000 | tf_op jit(solution)/shard_map/pallas_call | solution.py:555
  256.5 13.8 %all-to-all-start.2 = ((bf16[16,80,384]{2,1,0:T(8,128)(2,1)}), bf16[16,80,384]{2,1,0:T(8,128)(2,1)S(1)}, u32[]{:S(2)}, u32[]{:S(2)}) async-start(bf16[16,80,384]{2,1,0:T(8,128)(2,1)} %pad_maximum_fusion.4), calls=%async_computation.2 | async-start | bytes 1966080 | tf_op jit(solution)/shard_map/all_to_all | solution.py:713
  281.6 7.4 %all-to-all-done.2 = bf16[16,80,384]{2,1,0:T(8,128)(2,1)S(1)} async-done(((bf16[16,80,384]{2,1,0:T(8,128)(2,1)}), bf16[16,80,384]{2,1,0:T(8,128)(2,1)S(1)}, u32[]{:S(2)}, u32[]{:S(2)}) %all-to-all-start.2) | async-done | bytes 983072 | tf_op jit(solution)/shard_map/all_to_all | solution.py:713
  300.7 6.5 %collective-permute-done.27 = bf16[128,1024]{1,0:T(8,128)(2,1)S(1)} collective-permute-done((bf16[128,1024]{1,0:T(8,128)(2,1)S(1)}, bf16[128,1024]{1,0:T(8,128)(2,1)S(1)}, u32[]{:S(2)}, u32[]{:S(2)}) %collective-permute-start.27) | collective-permute-done | bytes 262176 | tf_op jit(solution)/shard_map/ppermute | solution.py:36
  314.3 12.6 %all_to_all.20.same_ref = bf16[8,80,384]{2,1,0:T(8,128)(2,1)S(1)} all-to-all(bf16[8,80,384]{2,1,0:T(8,128)(2,1)S(1)} %broadcast_in_dim.73), channel_id=1, replica_groups=mesh['a'=2,'z'=4,'c'=2,'y'=4,'b'=2] {'a','z'}, dimensions={0} | all-to-all | bytes 983040 | tf_op jit(solution)/shard_map/all_to_all | solution.py:720
  (232 shorter events, 116.1 us)
Async XLA Ops:
  7.2 101.2 %all-gather.5.cloned.1.call-start = ((), (), s32[]{:S(2)}) async-start(), calls=%async_computation.4 | async-start | bytes 5308416 | tf_op jit(solution)/shard_map/all_gather | solution.py:627
  11.5 25.0 %collective-permute-start.2 = (bf16[128,1024]{1,0:T(8,128)(2,1)S(1)}, bf16[128,1024]{1,0:T(8,128)(2,1)S(1)}, u32[]{:S(2)}, u32[]{:S(2)}) collective-permute-start(bf16[128,1024]{1,0:T(8,128)(2,1)S(1)} %bitcast.97), channel_id=1, source_target_pairs={{0,48},{16,0},{32,16},{48,32},{1,49},{17,1},{33,17},{49,33},{2,50}... | collective-permute-start | bytes 786440 | tf_op jit(solution)/shard_map/ppermute | solution.py:36
  16.1 20.4 %collective-permute-start.1 = (bf16[128,1024]{1,0:T(8,128)(2,1)S(1)}, bf16[128,1024]{1,0:T(8,128)(2,1)S(1)}, u32[]{:S(2)}, u32[]{:S(2)}) collective-permute-start(bf16[128,1024]{1,0:T(8,128)(2,1)S(1)} %bitcast.98), channel_id=1, source_target_pairs={{0,32},{16,48},{32,0},{48,16},{1,33},{17,49},{33,1},{49,17},{2,34}... | collective-permute-start | bytes 786440 | tf_op jit(solution)/shard_map/ppermute | solution.py:36
  16.1 20.4 %collective-permute-start = (bf16[128,1024]{1,0:T(8,128)(2,1)S(1)}, bf16[128,1024]{1,0:T(8,128)(2,1)S(1)}, u32[]{:S(2)}, u32[]{:S(2)}) collective-permute-start(bf16[128,1024]{1,0:T(8,128)(2,1)S(1)} %bitcast.99), channel_id=1, source_target_pairs={{0,16},{16,32},{32,48},{48,0},{1,17},{17,33},{33,49},{49,1},{2,18}... | collective-permute-start | bytes 786440 | tf_op jit(solution)/shard_map/ppermute | solution.py:36
  20.5 24.0 %all-to-all-start = ((bf16[8,144,256]{2,1,0:T(8,128)(2,1)}), bf16[8,144,256]{2,1,0:T(8,128)(2,1)S(1)}, u32[]{:S(2)}, u32[]{:S(2)}) async-start(bf16[8,144,256]{2,1,0:T(8,128)(2,1)} %broadcast_in_dim.64), calls=%async_computation | async-start | bytes 1179648 | tf_op jit(solution)/shard_map/all_to_all | solution.py:606
  27.1 68.1 %collective-permute-start.11 = (bf16[576,1024]{1,0:T(8,128)(2,1)}, bf16[576,1024]{1,0:T(8,128)(2,1)}, u32[]{:S(2)}, u32[]{:S(2)}) collective-permute-start(bf16[576,1024]{1,0:T(8,128)(2,1)} %param.25), channel_id=1, source_target_pairs={{0,0},{8,1},{16,2},{24,3},{32,4},{40,5},{48,6},{56,7},{1,8},{9,9},... | collective-permute-start | bytes 3538952 | tf_op jit(solution)/shard_map/ppermute | solution.py:84
  54.0 24.6 %collective-permute-start.10 = (bf16[128,1024]{1,0:T(8,128)(2,1)S(1)}, bf16[128,1024]{1,0:T(8,128)(2,1)S(1)}, u32[]{:S(2)}, u32[]{:S(2)}) collective-permute-start(bf16[128,1024]{1,0:T(8,128)(2,1)S(1)} %bitcast.102), channel_id=1, source_target_pairs={{0,48},{16,0},{32,16},{48,32},{1,49},{17,1},{33,17},{49,33},{2,50}... | collective-permute-start | bytes 786440 | tf_op jit(solution)/shard_map/ppermute | solution.py:36
  55.7 23.3 %collective-permute-start.9 = (bf16[128,1024]{1,0:T(8,128)(2,1)S(1)}, bf16[128,1024]{1,0:T(8,128)(2,1)S(1)}, u32[]{:S(2)}, u32[]{:S(2)}) collective-permute-start(bf16[128,1024]{1,0:T(8,128)(2,1)S(1)} %bitcast.103), channel_id=1, source_target_pairs={{0,32},{16,48},{32,0},{48,16},{1,33},{17,49},{33,1},{49,17},{2,34}... | collective-permute-start | bytes 786440 | tf_op jit(solution)/shard_map/ppermute | solution.py:36
  56.1 23.6 %collective-permute-start.8 = (bf16[128,1024]{1,0:T(8,128)(2,1)S(1)}, bf16[128,1024]{1,0:T(8,128)(2,1)S(1)}, u32[]{:S(2)}, u32[]{:S(2)}) collective-permute-start(bf16[128,1024]{1,0:T(8,128)(2,1)S(1)} %bitcast.104), channel_id=1, source_target_pairs={{0,16},{16,32},{32,48},{48,0},{1,17},{17,33},{33,49},{49,1},{2,18}... | collective-permute-start | bytes 786440 | tf_op jit(solution)/shard_map/ppermute | solution.py:36
  79.0 15.1 %collective-permute-start.5 = (bf16[1024,128]{1,0:T(8,128)(2,1)S(1)}, bf16[1024,128]{1,0:T(8,128)(2,1)S(1)}, u32[]{:S(2)}, u32[]{:S(2)}) collective-permute-start(bf16[1024,128]{1,0:T(8,128)(2,1)S(1)} %get-tuple-element.68.att_ref), channel_id=1, source_target_pairs={{0,16},{16,32},{32,48},{48,0},{1,17},{17,33},{33,49},{49,1},{2,18}... | collective-permute-start | bytes 786440 | tf_op jit(solution)/shard_map/ppermute | solution.py:36
  132.6 21.0 %collective-permute-start.14 = (bf16[512,1024]{1,0:T(8,128)(2,1)}, bf16[512,1024]{1,0:T(8,128)(2,1)}, u32[]{:S(2)}, u32[]{:S(2)}) collective-permute-start(bf16[512,1024]{1,0:T(8,128)(2,1)} %get-tuple-element.75), channel_id=1, source_target_pairs={{0,8},{8,0},{1,9},{9,1},{2,10},{10,2},{3,11},{11,3},{4,12},{12,4},... | collective-permute-start | bytes 3145736 | tf_op jit(solution)/shard_map/ppermute | solution.py:36
  147.8 72.2 %all-to-all-start.1 = ((bf16[16,3,64,576]{3,2,1,0:T(8,128)(2,1)}), bf16[16,3,64,576]{3,2,1,0:T(8,128)(2,1)}, u32[]{:S(2)}, u32[]{:S(2)}) async-start(bf16[16,3,64,576]{3,2,1,0:T(8,128)(2,1)} %copy-done.3), calls=%async_computation.1 | async-start | bytes 7864320 | tf_op jit(solution)/shard_map/all_to_all | solution.py:667
  153.6 154.9 %all-gather.7.cloned.1.call-start = ((), (), s32[]{:S(2)}) async-start(), calls=%async_computation.5 | async-start | bytes 4177920 | tf_op jit(solution)/shard_map/all_gather | solution.py:689
  159.1 13.6 %collective-permute-start.17 = (bf16[128,1024]{1,0:T(8,128)(2,1)S(1)}, bf16[128,1024]{1,0:T(8,128)(2,1)S(1)}, u32[]{:S(2)}, u32[]{:S(2)}) collective-permute-start(bf16[128,1024]{1,0:T(8,128)(2,1)S(1)} %get-tuple-element.131), channel_id=1, source_target_pairs={{0,16},{16,32},{32,48},{48,0},{1,17},{17,33},{33,49},{49,1},{2,18}... | collective-permute-start | bytes 786440 | tf_op jit(solution)/shard_map/ppermute | solution.py:36
  175.2 14.3 %collective-permute-start.18 = (bf16[128,1024]{1,0:T(8,128)(2,1)S(1)}, bf16[128,1024]{1,0:T(8,128)(2,1)S(1)}, u32[]{:S(2)}, u32[]{:S(2)}) collective-permute-start(bf16[128,1024]{1,0:T(8,128)(2,1)S(1)} %get-tuple-element.121), channel_id=1, source_target_pairs={{0,16},{16,32},{32,48},{48,0},{1,17},{17,33},{33,49},{49,1},{2,18}... | collective-permute-start | bytes 786440 | tf_op jit(solution)/shard_map/ppermute | solution.py:36
  217.4 16.1 %collective-permute-start.22 = (bf16[1024,128]{1,0:T(8,128)(2,1)}, bf16[1024,128]{1,0:T(8,128)(2,1)}, u32[]{:S(2)}, u32[]{:S(2)}) collective-permute-start(bf16[1024,128]{1,0:T(8,128)(2,1)} %get-tuple-element.86), channel_id=1, source_target_pairs={{0,64},{64,0},{1,65},{65,1},{2,66},{66,2},{3,67},{67,3},{4,68},{68... | collective-permute-start | bytes 786440 | tf_op jit(solution)/shard_map/ppermute | solution.py:36
  253.8 23.9 %collective-permute-start.24 = (bf16[512,1024]{1,0:T(8,128)(2,1)}, bf16[512,1024]{1,0:T(8,128)(2,1)S(1)}, u32[]{:S(2)}, u32[]{:S(2)}) collective-permute-start(bf16[512,1024]{1,0:T(8,128)(2,1)} %get-tuple-element.95), channel_id=1, source_target_pairs={{0,8},{8,0},{1,9},{9,1},{2,10},{10,2},{3,11},{11,3},{4,12},{12,4},... | collective-permute-start | bytes 3145736 | tf_op jit(solution)/shard_map/ppermute | solution.py:36
  256.5 32.6 %all-to-all-start.2 = ((bf16[16,80,384]{2,1,0:T(8,128)(2,1)}), bf16[16,80,384]{2,1,0:T(8,128)(2,1)S(1)}, u32[]{:S(2)}, u32[]{:S(2)}) async-start(bf16[16,80,384]{2,1,0:T(8,128)(2,1)} %pad_maximum_fusion.4), calls=%async_computation.2 | async-start | bytes 1966080 | tf_op jit(solution)/shard_map/all_to_all | solution.py:713
  275.0 17.9 %collective-permute-start.32 = (bf16[128,1024]{1,0:T(8,128)(2,1)}, bf16[128,1024]{1,0:T(8,128)(2,1)}, u32[]{:S(2)}, u32[]{:S(2)}) collective-permute-start(bf16[128,1024]{1,0:T(8,128)(2,1)} %get-tuple-element.126), channel_id=1, source_target_pairs={{0,16},{16,32},{32,48},{48,0},{1,17},{17,33},{33,49},{49,1},{2,18}... | collective-permute-start | bytes 786440 | tf_op jit(solution)/shard_map/ppermute | solution.py:36
  275.1 20.7 %collective-permute-start.31 = (bf16[128,1024]{1,0:T(8,128)(2,1)S(1)}, bf16[128,1024]{1,0:T(8,128)(2,1)}, u32[]{:S(2)}, u32[]{:S(2)}) collective-permute-start(bf16[128,1024]{1,0:T(8,128)(2,1)S(1)} %get-tuple-element.127), channel_id=1, source_target_pairs={{0,32},{16,48},{32,0},{48,16},{1,33},{17,49},{33,1},{49,17},{2,34}... | collective-permute-start | bytes 786440 | tf_op jit(solution)/shard_map/ppermute | solution.py:36
  275.1 22.6 %collective-permute-start.30 = (bf16[128,1024]{1,0:T(8,128)(2,1)S(1)}, bf16[128,1024]{1,0:T(8,128)(2,1)}, u32[]{:S(2)}, u32[]{:S(2)}) collective-permute-start(bf16[128,1024]{1,0:T(8,128)(2,1)S(1)} %get-tuple-element.125), channel_id=1, source_target_pairs={{0,48},{16,0},{32,16},{48,32},{1,49},{17,1},{33,17},{49,33},{2,50}... | collective-permute-start | bytes 786440 | tf_op jit(solution)/shard_map/ppermute | solution.py:36
  289.2 10.6 %collective-permute-start.25 = (bf16[80,128]{1,0:T(8,128)(2,1)S(1)}, bf16[80,128]{1,0:T(8,128)(2,1)S(1)}, u32[]{:S(2)}, u32[]{:S(2)}) collective-permute-start(bf16[80,128]{1,0:T(8,128)(2,1)S(1)} %slice.142), channel_id=1, source_target_pairs={{0,0},{1,8},{2,16},{3,24},{4,32},{5,40},{6,48},{7,56},{8,1},{9,9},... | collective-permute-start | bytes 61448 | tf_op jit(solution)/shard_map/ppermute | solution.py:76
  292.9 14.3 %collective-permute-start.27 = (bf16[128,1024]{1,0:T(8,128)(2,1)S(1)}, bf16[128,1024]{1,0:T(8,128)(2,1)S(1)}, u32[]{:S(2)}, u32[]{:S(2)}) collective-permute-start(bf16[128,1024]{1,0:T(8,128)(2,1)S(1)} %get-tuple-element.130), channel_id=1, source_target_pairs={{0,32},{16,48},{32,0},{48,16},{1,33},{17,49},{33,1},{49,17},{2,34}... | collective-permute-start | bytes 786440 | tf_op jit(solution)/shard_map/ppermute | solution.py:36
  295.8 11.4 %collective-permute-start.26 = (bf16[128,1024]{1,0:T(8,128)(2,1)S(1)}, bf16[128,1024]{1,0:T(8,128)(2,1)S(1)}, u32[]{:S(2)}, u32[]{:S(2)}) collective-permute-start(bf16[128,1024]{1,0:T(8,128)(2,1)S(1)} %get-tuple-element.128), channel_id=1, source_target_pairs={{0,48},{16,0},{32,16},{48,32},{1,49},{17,1},{33,17},{49,33},{2,50}... | collective-permute-start | bytes 786440 | tf_op jit(solution)/shard_map/ppermute | solution.py:36
  (55 other events, 513.1 us)
Sparse Core Ops, SparseCore 0:
  11.6 96.8 all-gather.4
  233.6 44.2 all-gather.6
where the time goes:
time: 342 us; the launch traced here: 341 us
  Pallas kernels  89.6 us (26%)
  starting transfers between devices  78.9 us (23%)
  waiting for transfers between devices  76.6 us (22%)
  local copies, waits for them, and re-layouts  31.2 us (9%)
  other arithmetic  28.8 us (8%)
  between operations  15.5 us (5%)
  blocking collectives  12.6 us (4%)
  matrix products  7.42 us (2%)
    ppermute x31, waiting for transfers between devices, shift(): lax.ppermute(value, axis, [(i, (i + step) % size) for i in range(size)])  59.3 us
    ppermute x31, starting transfers between devices, shift(): lax.ppermute(value, axis, [(i, (i + step) % size) for i in range(size)])  37.5 us
    pallas_call x1, Pallas kernels, ffn(): pl.pallas_call(ffn_kernel, grid=(HALF // rows,), in_specs=[SMEM, first, l...  23.1 us
    pallas_call x1, Pallas kernels, attention_backward(): pl.pallas_call(attention_backward_kernel, out_shape=(jax.ShapeDtypeStruct...  20.1 us
    unnamed x84, local copies, waits for them, and re-layouts  18.2 us
    pallas_call x1, Pallas kernels, attention_forward(): pl.pallas_call(attention_forward_kernel, out_shape=(jax.ShapeDtypeStruct(...  16.4 us
    all_to_all x1, starting transfers between devices, per_device(): lax.all_to_all(terms, ('y', 'b', 'a'), split_axis=0, concat_axis=0, tiled...  13.8 us
    all_to_all x1, blocking collectives, per_device(): lax.all_to_all(jnp.broadcast_to(piece[None], (8, 80, 384)), ('a', 'z'), s...  12.6 us
  transfers between devices with their start and end apart: 39, of which 19 were waited for; matrix products, arithmetic and copies ran while one was open for 13% of the time, Pallas kernels for 18%

commit v1 on v0

--- a/solution.py
+++ b/solution.py
@@ -84,7 +84,7 @@
     return lax.ppermute(value, ("z", "c", "y", "b"), pairs)
 
 
-KC = 256
+KC = 512
 
 
 def sort_keys(kb_ref, own_ref, peer_ref, keys, values, values_one):

time: 342 us -> 336 us (0.982)
  Pallas kernels: 89.6 us -> 82.5 us
  waiting for transfers between devices: 76.6 us -> 82.9 us
  starting transfers between devices: 78.9 us -> 73.1 us
    pallas_call x1, Pallas kernels: 20.1 us -> 16.6 us  [attention_backward(): pl.pallas_call(attention_backward_kernel, out_shape=(jax.ShapeDtypeStruct...]
    all_gather x1, waiting for transfers between devices: 8.67 us -> 12.2 us  [per_device(): wide = lax.all_gather(wide_own, FS, axis=0)]
    pallas_call x1, Pallas kernels: 16.4 us -> 12.9 us  [attention_forward(): pl.pallas_call(attention_forward_kernel, out_shape=(jax.ShapeDtypeStruct(...]
  transfers between devices with their start and end apart: 39 -> 39, of which waited for: 19 -> 19; matrix products, arithmetic and copies ran while one was open for 13% -> 14% of each run, Pallas kernels for 18% -> 16%
where the time goes in v1:
time: 336 us; the launch traced here: 334 us
  waiting for transfers between devices  82.9 us (25%)
  Pallas kernels  82.5 us (25%)
  starting transfers between devices  73.1 us (22%)
  local copies, waits for them, and re-layouts  31.2 us (9%)
  other arithmetic  28.8 us (9%)
  between operations  15.4 us (5%)
  blocking collectives  13 us (4%)
  matrix products  7.42 us (2%)
    ppermute x31, waiting for transfers between devices, shift(): lax.ppermute(value, axis, [(i, (i + step) % size) for i in range(size)])  60.6 us
    ppermute x31, starting transfers between devices, shift(): lax.ppermute(value, axis, [(i, (i + step) % size) for i in range(size)])  37.3 us
    pallas_call x1, Pallas kernels, ffn(): pl.pallas_call(ffn_kernel, grid=(HALF // rows,), in_specs=[SMEM, first, l...  23.1 us
    unnamed x84, local copies, waits for them, and re-layouts  18.2 us
    pallas_call x1, Pallas kernels, attention_backward(): pl.pallas_call(attention_backward_kernel, out_shape=(jax.ShapeDtypeStruct...  16.6 us
    all_to_all x1, blocking collectives, per_device(): lax.all_to_all(jnp.broadcast_to(piece[None], (8, 80, 384)), ('a', 'z'), s...  13 us
    pallas_call x1, Pallas kernels, attention_forward(): pl.pallas_call(attention_forward_kernel, out_shape=(jax.ShapeDtypeStruct(...  12.9 us
    all_gather x1, waiting for transfers between devices, per_device(): wide = lax.all_gather(wide_own, FS, axis=0)  12.2 us
  transfers between devices with their start and end apart: 39, of which 19 were waited for; matrix products, arithmetic and copies ran while one was open for 14% of the time, Pallas kernels for 16%

profile of v1, /device:TPU:1, one launch (start us, length us, event | category | flops | bytes accessed | tf_op | source)
XLA Modules:
  0.0 334.5 jit_solution(17893768876984907904)
XLA Ops:
  11.5 4.6 %collective-permute-start.2 = (bf16[128,1024]{1,0:T(8,128)(2,1)S(1)}, bf16[128,1024]{1,0:T(8,128)(2,1)S(1)}, u32[]{:S(2)}, u32[]{:S(2)}) collective-permute-start(bf16[128,1024]{1,0:T(8,128)(2,1)S(1)} %bitcast.97), channel_id=1, source_target_pairs={{0,48},{16,0},{32,16},{48,32},{1,49},{17,1},{33,17},{49,33},{2,50}... | collective-permute-start | bytes 786440 | tf_op jit(solution)/shard_map/ppermute | solution.py:36
  20.5 6.7 %all-to-all-start = ((bf16[8,144,256]{2,1,0:T(8,128)(2,1)}), bf16[8,144,256]{2,1,0:T(8,128)(2,1)S(1)}, u32[]{:S(2)}, u32[]{:S(2)}) async-start(bf16[8,144,256]{2,1,0:T(8,128)(2,1)} %broadcast_in_dim.64), calls=%async_computation | async-start | bytes 1179648 | tf_op jit(solution)/shard_map/all_to_all | solution.py:606
  27.1 6.8 %collective-permute-start.11 = (bf16[576,1024]{1,0:T(8,128)(2,1)}, bf16[576,1024]{1,0:T(8,128)(2,1)}, u32[]{:S(2)}, u32[]{:S(2)}) collective-permute-start(bf16[576,1024]{1,0:T(8,128)(2,1)} %param.25), channel_id=1, source_target_pairs={{0,0},{8,1},{16,2},{24,3},{32,4},{40,5},{48,6},{56,7},{1,8},{9,9},... | collective-permute-start | bytes 3538952 | tf_op jit(solution)/shard_map/ppermute | solution.py:84
  36.7 5.4 %collective-permute-start.3 = (bf16[512,1024]{1,0:T(8,128)(2,1)S(1)}, bf16[512,1024]{1,0:T(8,128)(2,1)}, u32[]{:S(2)}, u32[]{:S(2)}) collective-permute-start(bf16[512,1024]{1,0:T(8,128)(2,1)S(1)} %pad_maximum_fusion.x_ref), channel_id=1, source_target_pairs={{0,8},{8,0},{1,9},{9,1},{2,10},{10,2},{3,11},{11,3},{4,12},{12,4},... | collective-permute-start | bytes 3145736 | tf_op jit(solution)/shard_map/ppermute | solution.py:36
  45.3 7.4 %shard_map.246 = (f32[1024,256]{1,0:T(8,128)S(1)}, bf16[2,1024,64]{2,1,0:T(8,128)(2,1)S(1)}, bf16[1024,128]{1,0:T(8,128)(2,1)S(1)}) custom-call(bf16[512,1024]{1,0:T(8,128)(2,1)S(1)} %pad_maximum_fusion.x_ref, bf16[512,1024]{1,0:T(8,128)(2,1)} %collective-permute-done.3.x_other_ref, bf16[8,144,256]{2,1,0:T(8,128)(2,1)S(1)} %all-to-all-done.weights_ref, ...), custom_call_target="tpu_custom_call" | custom-call | flops 500000000 | bytes 4000000 | tf_op jit(solution)/shard_map/pallas_call | solution.py:484
  56.8 4.7 %collective-permute-done.4.peer_ref = bf16[1024,128]{1,0:T(8,128)(2,1)S(1)} collective-permute-done((bf16[1024,128]{1,0:T(8,128)(2,1)S(1)}, bf16[1024,128]{1,0:T(8,128)(2,1)S(1)}, u32[]{:S(2)}, u32[]{:S(2)}) %collective-permute-start.4) | collective-permute-done | bytes 262176 | tf_op jit(solution)/shard_map/ppermute | solution.py:36
  61.4 12.9 %shard_map.247 = (bf16[1024,128]{1,0:T(8,128)(2,1)S(1)}, f32[128,128]{1,0:T(8,128)S(1)}) custom-call(s32[32]{0:T(128)S(1)} %select_reduce_fusion.kb_ref, s32[1]{0:T(128)} %copy.48.split_ref, bf16[2,1024,64]{2,1,0:T(8,128)(2,1)S(1)} %get-tuple-element.66.q_ref, bf16[1024,128]{1,0:T(8,128)(2,1)S(1)} %get-tuple-element.67.own_ref, ...), custom_call_target="tpu_custom_call" | custom-call | flops 500000000 | bytes 2000000 | tf_op jit(solution)/shard_map/pallas_call | solution.py:144
  77.3 4.1 %collective-permute-done.7 = bf16[1024,128]{1,0:T(8,128)(2,1)S(1)} collective-permute-done((bf16[1024,128]{1,0:T(8,128)(2,1)S(1)}, bf16[1024,128]{1,0:T(8,128)(2,1)S(1)}, u32[]{:S(2)}, u32[]{:S(2)}) %collective-permute-start.7) | collective-permute-done | bytes 262176 | tf_op jit(solution)/shard_map/ppermute | solution.py:36
  82.4 8.2 %collective-permute-done.5 = bf16[1024,128]{1,0:T(8,128)(2,1)S(1)} collective-permute-done((bf16[1024,128]{1,0:T(8,128)(2,1)S(1)}, bf16[1024,128]{1,0:T(8,128)(2,1)S(1)}, u32[]{:S(2)}, u32[]{:S(2)}) %collective-permute-start.5) | collective-permute-done | bytes 262176 | tf_op jit(solution)/shard_map/ppermute | solution.py:36
  96.3 12.2 %all-gather.5.cloned.1.call-done = bf16[1024,2240]{1,0:T(8,128)(2,1)} async-done(((bf16[128,2240]{1,0:T(8,128)(2,1)}), bf16[1024,2240]{1,0:T(8,128)(2,1)}) %all-gather.5.cloned.1.call-update) | async-done | bytes 4587536 | tf_op jit(solution)/shard_map/all_gather | solution.py:627
  108.6 23.1 %shard_map.248 = (bf16[1024,1024]{1,0:T(8,128)(2,1)}, bf16[1024,576]{1,0:T(8,128)(2,1)}, bf16[1024,576]{1,0:T(8,128)(2,1)}, bf16[1024,576]{1,0:T(8,128)(2,1)}, f...) custom-call(s32[8]{0:T(128)S(1)} %stack.182.order_ref, ...), custom_call_target="tpu_custom_call" | custom-call | flops 11000000512 | bytes 24000000 | tf_op jit(solution)/shard_map/pallas_call | solution.py:307
  139.2 6.6 %shard_map.249 = bf16[16,3,64,576]{3,2,1,0:T(8,128)(2,1)S(1)} custom-call(bf16[1024,1024]{1,0:T(8,128)(2,1)S(1)} %copy-done.23, bf16[512,1024]{1,0:T(8,128)(2,1)} %pad_maximum_fusion.2.cot_ref, bf16[512,1024]{1,0:T(8,128)(2,1)} %collective-permute-done.13.cot_other_ref, bf16[1024,576]{1,0:T(8,128)(2,1)S(1)} %copy-done.24, bf16[1024,576]{1,0:T(8,128)(2,1)S(1)} %copy-done.25, ...), custom_call_target="tpu_custom_call" | custom-call | flops 4000000000 | bytes 11000000 | tf_op jit(solution)/shard_map/pallas_call | solution.py:349
  147.8 4.5 %all-to-all-start.1 = ((bf16[16,3,64,576]{3,2,1,0:T(8,128)(2,1)}), bf16[16,3,64,576]{3,2,1,0:T(8,128)(2,1)}, u32[]{:S(2)}, u32[]{:S(2)}) async-start(bf16[16,3,64,576]{3,2,1,0:T(8,128)(2,1)} %copy-done.3), calls=%async_computation.1 | async-start | bytes 7864320 | tf_op jit(solution)/shard_map/all_to_all | solution.py:667
  158.6 10.2 %collective-permute-done.15 = bf16[128,1024]{1,0:T(8,128)(2,1)S(1)} collective-permute-done((bf16[128,1024]{1,0:T(8,128)(2,1)S(1)}, bf16[128,1024]{1,0:T(8,128)(2,1)S(1)}, u32[]{:S(2)}, u32[]{:S(2)}) %collective-permute-start.15) | collective-permute-done | bytes 262176 | tf_op jit(solution)/shard_map/ppermute | solution.py:36
  168.8 4.2 %collective-permute-done.17 = bf16[128,1024]{1,0:T(8,128)(2,1)S(1)} collective-permute-done((bf16[128,1024]{1,0:T(8,128)(2,1)S(1)}, bf16[128,1024]{1,0:T(8,128)(2,1)S(1)}, u32[]{:S(2)}, u32[]{:S(2)}) %collective-permute-start.17) | collective-permute-done | bytes 262176 | tf_op jit(solution)/shard_map/ppermute | solution.py:36
  175.8 6.1 %collective-permute-done.20 = bf16[128,1024]{1,0:T(8,128)(2,1)S(1)} collective-permute-done((bf16[128,1024]{1,0:T(8,128)(2,1)S(1)}, bf16[128,1024]{1,0:T(8,128)(2,1)S(1)}, u32[]{:S(2)}, u32[]{:S(2)}) %collective-permute-start.20) | collective-permute-done | bytes 262176 | tf_op jit(solution)/shard_map/ppermute | solution.py:36
  182.8 7.0 %collective-permute-done.18 = bf16[128,1024]{1,0:T(8,128)(2,1)S(1)} collective-permute-done((bf16[128,1024]{1,0:T(8,128)(2,1)S(1)}, bf16[128,1024]{1,0:T(8,128)(2,1)S(1)}, u32[]{:S(2)}, u32[]{:S(2)}) %collective-permute-start.18) | collective-permute-done | bytes 262176 | tf_op jit(solution)/shard_map/ppermute | solution.py:36
  195.9 16.6 %shard_map.250 = (bf16[2,1024,64]{2,1,0:T(8,128)(2,1)S(1)}, f32[1024,128]{1,0:T(8,128)S(1)}, bf16[1024,128]{1,0:T(8,128)(2,1)}) custom-call(s32[32]{0:T(128)S(1)} %select_reduce_fusion.kb_ref, s32[1]{0:T(128)} %copy.48.split_ref, bf16[2,1024,64]{2,1,0:T(8,128)(2,1)S(1)} %copy-done.16, bf16[1024,128]{1,0:T(8,128)(2,1)S(1)} %copy-done.18, ...), custom_call_target="tpu_custom_call" | custom-call | flops 500000000 | bytes 4000000 | tf_op jit(solution)/shard_map/pallas_call | solution.py:215
  236.5 10.9 %shard_map.251 = (f32[512,1024]{1,0:T(8,128)S(1)}, bf16[512,1024]{1,0:T(8,128)(2,1)}, bf16[1024,256]{1,0:T(8,128)(2,1)S(1)}, f32[1,1024]{1,0:T(1,128)S(1)}, f32[1,64]{1,0:T(1,128)S(1)}, /*index=5*/f32[1,64]{1,0:T(1,128)S(1)}) custom-call(bf16[512,1024]{1,0:T(8,128)(2,1)S(1)} %pad_maximum_fusion.x_ref, bf16[512,1024]{1,0:T(8,128)(2,1)} %collective-permute-done.3.x_other_ref, ...), custom_call_target="tpu_custom_call" | custom-call | flops 1000000000 | bytes 6000000 | tf_op jit(solution)/shard_map/pallas_call | solution.py:555
  252.2 11.9 %all-to-all-start.2 = ((bf16[16,80,384]{2,1,0:T(8,128)(2,1)}), bf16[16,80,384]{2,1,0:T(8,128)(2,1)S(1)}, u32[]{:S(2)}, u32[]{:S(2)}) async-start(bf16[16,80,384]{2,1,0:T(8,128)(2,1)} %pad_maximum_fusion.4), calls=%async_computation.2 | async-start | bytes 1966080 | tf_op jit(solution)/shard_map/all_to_all | solution.py:713
  264.1 3.9 %fusion.26 = (bf16[512,1024]{1,0:T(8,128)(2,1)S(1)}, f32[512,1024]{1,0:T(8,128)}) fusion(f32[512,1024]{1,0:T(8,128)} %get-tuple-element.103, bf16[512,1024]{1,0:T(8,128)(2,1)} %collective-permute-done.29), kind=kLoop, calls=%fused_computation.83 | loop fusion | flops 1572864 | bytes 6291456 | tf_op jit(solution)/shard_map/convert_element_type | solution.py:60
  275.4 7.6 %all-to-all-done.2 = bf16[16,80,384]{2,1,0:T(8,128)(2,1)S(1)} async-done(((bf16[16,80,384]{2,1,0:T(8,128)(2,1)}), bf16[16,80,384]{2,1,0:T(8,128)(2,1)S(1)}, u32[]{:S(2)}, u32[]{:S(2)}) %all-to-all-start.2) | async-done | bytes 983072 | tf_op jit(solution)/shard_map/all_to_all | solution.py:713
  294.2 6.5 %collective-permute-done.27 = bf16[128,1024]{1,0:T(8,128)(2,1)S(1)} collective-permute-done((bf16[128,1024]{1,0:T(8,128)(2,1)S(1)}, bf16[128,1024]{1,0:T(8,128)(2,1)S(1)}, u32[]{:S(2)}, u32[]{:S(2)}) %collective-permute-start.27) | collective-permute-done | bytes 262176 | tf_op jit(solution)/shard_map/ppermute | solution.py:36
  307.8 13.0 %all_to_all.20.same_ref = bf16[8,80,384]{2,1,0:T(8,128)(2,1)S(1)} all-to-all(bf16[8,80,384]{2,1,0:T(8,128)(2,1)S(1)} %broadcast_in_dim.73), channel_id=1, replica_groups=mesh['a'=2,'z'=4,'c'=2,'y'=4,'b'=2] {'a','z'}, dimensions={0} | all-to-all | bytes 983040 | tf_op jit(solution)/shard_map/all_to_all | solution.py:720
  (232 shorter events, 113.9 us)
Async XLA Ops:
  7.2 101.3 %all-gather.5.cloned.1.call-start = ((), (), s32[]{:S(2)}) async-start(), calls=%async_computation.4 | async-start | bytes 5308416 | tf_op jit(solution)/shard_map/all_gather | solution.py:627
  11.5 25.0 %collective-permute-start.2 = (bf16[128,1024]{1,0:T(8,128)(2,1)S(1)}, bf16[128,1024]{1,0:T(8,128)(2,1)S(1)}, u32[]{:S(2)}, u32[]{:S(2)}) collective-permute-start(bf16[128,1024]{1,0:T(8,128)(2,1)S(1)} %bitcast.97), channel_id=1, source_target_pairs={{0,48},{16,0},{32,16},{48,32},{1,49},{17,1},{33,17},{49,33},{2,50}... | collective-permute-start | bytes 786440 | tf_op jit(solution)/shard_map/ppermute | solution.py:36
  16.1 20.4 %collective-permute-start.1 = (bf16[128,1024]{1,0:T(8,128)(2,1)S(1)}, bf16[128,1024]{1,0:T(8,128)(2,1)S(1)}, u32[]{:S(2)}, u32[]{:S(2)}) collective-permute-start(bf16[128,1024]{1,0:T(8,128)(2,1)S(1)} %bitcast.98), channel_id=1, source_target_pairs={{0,32},{16,48},{32,0},{48,16},{1,33},{17,49},{33,1},{49,17},{2,34}... | collective-permute-start | bytes 786440 | tf_op jit(solution)/shard_map/ppermute | solution.py:36
  16.1 20.4 %collective-permute-start = (bf16[128,1024]{1,0:T(8,128)(2,1)S(1)}, bf16[128,1024]{1,0:T(8,128)(2,1)S(1)}, u32[]{:S(2)}, u32[]{:S(2)}) collective-permute-start(bf16[128,1024]{1,0:T(8,128)(2,1)S(1)} %bitcast.99), channel_id=1, source_target_pairs={{0,16},{16,32},{32,48},{48,0},{1,17},{17,33},{33,49},{49,1},{2,18}... | collective-permute-start | bytes 786440 | tf_op jit(solution)/shard_map/ppermute | solution.py:36
  20.5 24.0 %all-to-all-start = ((bf16[8,144,256]{2,1,0:T(8,128)(2,1)}), bf16[8,144,256]{2,1,0:T(8,128)(2,1)S(1)}, u32[]{:S(2)}, u32[]{:S(2)}) async-start(bf16[8,144,256]{2,1,0:T(8,128)(2,1)} %broadcast_in_dim.64), calls=%async_computation | async-start | bytes 1179648 | tf_op jit(solution)/shard_map/all_to_all | solution.py:606
  27.1 64.6 %collective-permute-start.11 = (bf16[576,1024]{1,0:T(8,128)(2,1)}, bf16[576,1024]{1,0:T(8,128)(2,1)}, u32[]{:S(2)}, u32[]{:S(2)}) collective-permute-start(bf16[576,1024]{1,0:T(8,128)(2,1)} %param.25), channel_id=1, source_target_pairs={{0,0},{8,1},{16,2},{24,3},{32,4},{40,5},{48,6},{56,7},{1,8},{9,9},... | collective-permute-start | bytes 3538952 | tf_op jit(solution)/shard_map/ppermute | solution.py:84
  54.0 21.1 %collective-permute-start.10 = (bf16[128,1024]{1,0:T(8,128)(2,1)S(1)}, bf16[128,1024]{1,0:T(8,128)(2,1)S(1)}, u32[]{:S(2)}, u32[]{:S(2)}) collective-permute-start(bf16[128,1024]{1,0:T(8,128)(2,1)S(1)} %bitcast.102), channel_id=1, source_target_pairs={{0,48},{16,0},{32,16},{48,32},{1,49},{17,1},{33,17},{49,33},{2,50}... | collective-permute-start | bytes 786440 | tf_op jit(solution)/shard_map/ppermute | solution.py:36
  55.7 19.8 %collective-permute-start.9 = (bf16[128,1024]{1,0:T(8,128)(2,1)S(1)}, bf16[128,1024]{1,0:T(8,128)(2,1)S(1)}, u32[]{:S(2)}, u32[]{:S(2)}) collective-permute-start(bf16[128,1024]{1,0:T(8,128)(2,1)S(1)} %bitcast.103), channel_id=1, source_target_pairs={{0,32},{16,48},{32,0},{48,16},{1,33},{17,49},{33,1},{49,17},{2,34}... | collective-permute-start | bytes 786440 | tf_op jit(solution)/shard_map/ppermute | solution.py:36
  56.1 20.1 %collective-permute-start.8 = (bf16[128,1024]{1,0:T(8,128)(2,1)S(1)}, bf16[128,1024]{1,0:T(8,128)(2,1)S(1)}, u32[]{:S(2)}, u32[]{:S(2)}) collective-permute-start(bf16[128,1024]{1,0:T(8,128)(2,1)S(1)} %bitcast.104), channel_id=1, source_target_pairs={{0,16},{16,32},{32,48},{48,0},{1,17},{17,33},{33,49},{49,1},{2,18}... | collective-permute-start | bytes 786440 | tf_op jit(solution)/shard_map/ppermute | solution.py:36
  75.5 15.1 %collective-permute-start.5 = (bf16[1024,128]{1,0:T(8,128)(2,1)S(1)}, bf16[1024,128]{1,0:T(8,128)(2,1)S(1)}, u32[]{:S(2)}, u32[]{:S(2)}) collective-permute-start(bf16[1024,128]{1,0:T(8,128)(2,1)S(1)} %get-tuple-element.68.att_ref), channel_id=1, source_target_pairs={{0,16},{16,32},{32,48},{48,0},{1,17},{17,33},{33,49},{49,1},{2,18}... | collective-permute-start | bytes 786440 | tf_op jit(solution)/shard_map/ppermute | solution.py:36
  132.6 19.8 %collective-permute-start.14 = (bf16[512,1024]{1,0:T(8,128)(2,1)}, bf16[512,1024]{1,0:T(8,128)(2,1)}, u32[]{:S(2)}, u32[]{:S(2)}) collective-permute-start(bf16[512,1024]{1,0:T(8,128)(2,1)} %get-tuple-element.75), channel_id=1, source_target_pairs={{0,8},{8,0},{1,9},{9,1},{2,10},{10,2},{3,11},{11,3},{4,12},{12,4},... | collective-permute-start | bytes 3145736 | tf_op jit(solution)/shard_map/ppermute | solution.py:36
  147.8 69.0 %all-to-all-start.1 = ((bf16[16,3,64,576]{3,2,1,0:T(8,128)(2,1)}), bf16[16,3,64,576]{3,2,1,0:T(8,128)(2,1)}, u32[]{:S(2)}, u32[]{:S(2)}) async-start(bf16[16,3,64,576]{3,2,1,0:T(8,128)(2,1)} %copy-done.3), calls=%async_computation.1 | async-start | bytes 7864320 | tf_op jit(solution)/shard_map/all_to_all | solution.py:667
  152.4 149.6 %all-gather.7.cloned.1.call-start = ((), (), s32[]{:S(2)}) async-start(), calls=%async_computation.5 | async-start | bytes 4177920 | tf_op jit(solution)/shard_map/all_gather | solution.py:689
  154.8 14.0 %collective-permute-start.15 = (bf16[128,1024]{1,0:T(8,128)(2,1)S(1)}, bf16[128,1024]{1,0:T(8,128)(2,1)S(1)}, u32[]{:S(2)}, u32[]{:S(2)}) collective-permute-start(bf16[128,1024]{1,0:T(8,128)(2,1)S(1)} %get-tuple-element.133), channel_id=1, source_target_pairs={{0,48},{16,0},{32,16},{48,32},{1,49},{17,1},{33,17},{49,33},{2,50}... | collective-permute-start | bytes 786440 | tf_op jit(solution)/shard_map/ppermute | solution.py:36
  157.5 11.2 %collective-permute-start.16 = (bf16[128,1024]{1,0:T(8,128)(2,1)S(1)}, bf16[128,1024]{1,0:T(8,128)(2,1)S(1)}, u32[]{:S(2)}, u32[]{:S(2)}) collective-permute-start(bf16[128,1024]{1,0:T(8,128)(2,1)S(1)} %get-tuple-element.132), channel_id=1, source_target_pairs={{0,32},{16,48},{32,0},{48,16},{1,33},{17,49},{33,1},{49,17},{2,34}... | collective-permute-start | bytes 786440 | tf_op jit(solution)/shard_map/ppermute | solution.py:36
  157.9 15.1 %collective-permute-start.17 = (bf16[128,1024]{1,0:T(8,128)(2,1)S(1)}, bf16[128,1024]{1,0:T(8,128)(2,1)S(1)}, u32[]{:S(2)}, u32[]{:S(2)}) collective-permute-start(bf16[128,1024]{1,0:T(8,128)(2,1)S(1)} %get-tuple-element.131), channel_id=1, source_target_pairs={{0,16},{16,32},{32,48},{48,0},{1,17},{17,33},{33,49},{49,1},{2,18}... | collective-permute-start | bytes 786440 | tf_op jit(solution)/shard_map/ppermute | solution.py:36
  174.7 15.1 %collective-permute-start.18 = (bf16[128,1024]{1,0:T(8,128)(2,1)S(1)}, bf16[128,1024]{1,0:T(8,128)(2,1)S(1)}, u32[]{:S(2)}, u32[]{:S(2)}) collective-permute-start(bf16[128,1024]{1,0:T(8,128)(2,1)S(1)} %get-tuple-element.121), channel_id=1, source_target_pairs={{0,16},{16,32},{32,48},{48,0},{1,17},{17,33},{33,49},{49,1},{2,18}... | collective-permute-start | bytes 786440 | tf_op jit(solution)/shard_map/ppermute | solution.py:36
  214.0 15.2 %collective-permute-start.22 = (bf16[1024,128]{1,0:T(8,128)(2,1)}, bf16[1024,128]{1,0:T(8,128)(2,1)}, u32[]{:S(2)}, u32[]{:S(2)}) collective-permute-start(bf16[1024,128]{1,0:T(8,128)(2,1)} %get-tuple-element.86), channel_id=1, source_target_pairs={{0,64},{64,0},{1,65},{65,1},{2,66},{66,2},{3,67},{67,3},{4,68},{68... | collective-permute-start | bytes 786440 | tf_op jit(solution)/shard_map/ppermute | solution.py:36
  249.5 22.0 %collective-permute-start.24 = (bf16[512,1024]{1,0:T(8,128)(2,1)}, bf16[512,1024]{1,0:T(8,128)(2,1)S(1)}, u32[]{:S(2)}, u32[]{:S(2)}) collective-permute-start(bf16[512,1024]{1,0:T(8,128)(2,1)} %get-tuple-element.95), channel_id=1, source_target_pairs={{0,8},{8,0},{1,9},{9,1},{2,10},{10,2},{3,11},{11,3},{4,12},{12,4},... | collective-permute-start | bytes 3145736 | tf_op jit(solution)/shard_map/ppermute | solution.py:36
  252.2 30.8 %all-to-all-start.2 = ((bf16[16,80,384]{2,1,0:T(8,128)(2,1)}), bf16[16,80,384]{2,1,0:T(8,128)(2,1)S(1)}, u32[]{:S(2)}, u32[]{:S(2)}) async-start(bf16[16,80,384]{2,1,0:T(8,128)(2,1)} %pad_maximum_fusion.4), calls=%async_computation.2 | async-start | bytes 1966080 | tf_op jit(solution)/shard_map/all_to_all | solution.py:713
  268.8 17.9 %collective-permute-start.32 = (bf16[128,1024]{1,0:T(8,128)(2,1)}, bf16[128,1024]{1,0:T(8,128)(2,1)}, u32[]{:S(2)}, u32[]{:S(2)}) collective-permute-start(bf16[128,1024]{1,0:T(8,128)(2,1)} %get-tuple-element.126), channel_id=1, source_target_pairs={{0,16},{16,32},{32,48},{48,0},{1,17},{17,33},{33,49},{49,1},{2,18}... | collective-permute-start | bytes 786440 | tf_op jit(solution)/shard_map/ppermute | solution.py:36
  268.8 20.8 %collective-permute-start.31 = (bf16[128,1024]{1,0:T(8,128)(2,1)S(1)}, bf16[128,1024]{1,0:T(8,128)(2,1)}, u32[]{:S(2)}, u32[]{:S(2)}) collective-permute-start(bf16[128,1024]{1,0:T(8,128)(2,1)S(1)} %get-tuple-element.127), channel_id=1, source_target_pairs={{0,32},{16,48},{32,0},{48,16},{1,33},{17,49},{33,1},{49,17},{2,34}... | collective-permute-start | bytes 786440 | tf_op jit(solution)/shard_map/ppermute | solution.py:36
  268.8 22.6 %collective-permute-start.30 = (bf16[128,1024]{1,0:T(8,128)(2,1)S(1)}, bf16[128,1024]{1,0:T(8,128)(2,1)}, u32[]{:S(2)}, u32[]{:S(2)}) collective-permute-start(bf16[128,1024]{1,0:T(8,128)(2,1)S(1)} %get-tuple-element.125), channel_id=1, source_target_pairs={{0,48},{16,0},{32,16},{48,32},{1,49},{17,1},{33,17},{49,33},{2,50}... | collective-permute-start | bytes 786440 | tf_op jit(solution)/shard_map/ppermute | solution.py:36
  286.7 13.9 %collective-permute-start.27 = (bf16[128,1024]{1,0:T(8,128)(2,1)S(1)}, bf16[128,1024]{1,0:T(8,128)(2,1)S(1)}, u32[]{:S(2)}, u32[]{:S(2)}) collective-permute-start(bf16[128,1024]{1,0:T(8,128)(2,1)S(1)} %get-tuple-element.130), channel_id=1, source_target_pairs={{0,32},{16,48},{32,0},{48,16},{1,33},{17,49},{33,1},{49,17},{2,34}... | collective-permute-start | bytes 786440 | tf_op jit(solution)/shard_map/ppermute | solution.py:36
  (55 other events, 509.1 us)
Sparse Core Ops, SparseCore 0:
  11.6 96.9 all-gather.4
  229.4 42.2 all-gather.6
